TPU v7x, 32 devices: a whole 2x2x4 slice. The times are simulated.
32 devices in a mesh: exp: 8 (over y, x, core), seq: 4 (over z).
Axes of the slice: x: 2, y: 2, z: 4, core: 2. Of those that a mesh axis runs over, the one named last changes fastest.
Arguments:
- projected: bfloat16 [8, 512, 3, 16, 128], P('exp', 'seq'), may hold values from -5 to 5
- hidden_in: bfloat16 [8, 512, 2048], P('exp', 'seq'), may hold values from -6 to 6
- modulation: float32 [8, 4, 2048], P('exp'), may hold values from -4 to 4
- w_router: bfloat16 [2048, 8], replicated, may hold values from -0.125 to 0.125
- picked: int32 [8, 4, 8, 2], P('exp', 'seq'), may hold values from 0 to 511, as said below
- counts: int32 [8, 4, 8], P('exp', 'seq'), may hold values from 0 to 2, as said below
- weight_in: bfloat16 [8, 2048, 4096], P('exp', None, 'seq'), may hold values from -0.125 to 0.125
- weight_out: bfloat16 [8, 4096, 2048], P('exp', 'seq'), may hold values from -0.09375 to 0.09375
Outputs:
- layer_out: bfloat16 [8, 512, 2048], P('exp', 'seq')
Inputs may be any that keep to these rules, and one draw needn't show every extreme that they name: picked[i, s, e, c] lies in shard s of image i, from s * 128 to s * 128 + 127; the entries of one block are distinct. `counts`: in every draw one expert has 2 live slots in every block, and every device's tokens fill all 2 slots of some expert.
All inputs are finite; a program needn't handle non-finite values.
Results may differ from a plain program's by a relative error of at most 0.007.
Values may be sent and summed in bfloat16 or wider, within the bound.
A program may use at most 64 MiB of HBM per device.

v0:
```python
import math

import jax
import jax.numpy as jnp
from jax import lax
from jax.sharding import PartitionSpec as P

epsilon_norm = 1e-06


def attend_head(queries, keys_all, values_all):
    length = queries.shape[0]
    block_size = min(512, length)
    score_scale = 1.0 / math.sqrt(queries.shape[1])

    def one_block(query_rows):
        scores = jnp.dot(query_rows, keys_all.T, preferred_element_type=jnp.float32) * score_scale
        top_score = jnp.max(scores, axis=-1, keepdims=True)
        weights = jnp.exp(scores - top_score)
        weights = weights / jnp.sum(weights, axis=-1, keepdims=True)
        return jnp.dot(
            weights.astype(jnp.bfloat16), values_all, preferred_element_type=jnp.float32
        ).astype(jnp.bfloat16)

    blocked = queries.reshape(length // block_size, block_size, queries.shape[1])
    return lax.map(one_block, blocked).reshape(length, queries.shape[1])


def head_attention(head_data):
    return attend_head(head_data[:, 0], head_data[:, 1], head_data[:, 2])


def modulate(residual, shift_row, scale_row):
    average = jnp.mean(residual, axis=-1, keepdims=True)
    centred = residual - average
    variance = jnp.mean(centred * centred, axis=-1, keepdims=True)
    normed = centred * lax.rsqrt(variance + epsilon_norm)
    return (normed * (1.0 + scale_row) + shift_row).astype(jnp.bfloat16)


def per_device(projected, hidden_in, modulation, w_router, picked, counts, weight_in, weight_out):
    tok_count = hidden_in.shape[1]
    model_width = hidden_in.shape[2]
    gathered = lax.all_to_all(projected, "seq", split_axis=3, concat_axis=1, tiled=True)
    per_head = jnp.moveaxis(gathered[0], 2, 0)
    attended = lax.map(head_attention, per_head)
    attended = jnp.moveaxis(attended, 0, 1)[None]
    returned = lax.all_to_all(attended, "seq", split_axis=1, concat_axis=2, tiled=True)
    attn_rows = returned.reshape(tok_count, model_width)
    conditioning = modulation[0]
    residual = hidden_in[0].astype(jnp.float32) + conditioning[0] * attn_rows.astype(jnp.float32)
    modulated = modulate(residual, conditioning[1], conditioning[2])
    gate_values = jax.nn.sigmoid(jnp.dot(modulated, w_router, preferred_element_type=jnp.float32))
    expert_count = w_router.shape[1]
    capacity = picked.shape[3]
    local_pos = picked[0, 0] - lax.axis_index("seq") * tok_count
    live_slots = (
        lax.broadcasted_iota(jnp.int32, (expert_count, capacity), 1) < counts[0, 0][:, None]
    )
    token_ids = lax.broadcasted_iota(jnp.int32, (expert_count, capacity, tok_count), 2)
    selector = (local_pos[:, :, None] == token_ids) & live_slots[:, :, None]
    dispatch_rows = jnp.dot(
        selector.astype(jnp.bfloat16).reshape(expert_count * capacity, tok_count),
        modulated,
        preferred_element_type=jnp.float32,
    )
    dispatch_rows = dispatch_rows.astype(jnp.bfloat16).reshape(expert_count, capacity, model_width)
    arrived = lax.all_to_all(dispatch_rows, "exp", split_axis=0, concat_axis=0, tiled=True)
    expert_in = weight_in[0]
    expert_out = weight_out[0]
    product = jnp.einsum(
        "ncd,df->ncf",
        lax.all_gather(arrived, "seq", axis=0, tiled=True),
        expert_in,
        preferred_element_type=jnp.float32,
    )
    hidden = jax.nn.gelu(product, approximate=True).astype(jnp.bfloat16)
    summed = lax.psum_scatter(
        jnp.einsum("ncf,fd->ncd", hidden, expert_out, preferred_element_type=jnp.float32).astype(
            jnp.bfloat16
        ),
        "seq",
        scatter_dimension=0,
        tiled=True,
    )
    expert_rows = lax.all_to_all(summed, "exp", split_axis=0, concat_axis=0, tiled=True)
    slot_weight = selector.astype(jnp.float32) * gate_values.T[:, None, :]
    mixture = jnp.einsum(
        "ect,ecd->td", slot_weight, expert_rows.astype(jnp.float32), precision=lax.Precision.HIGHEST
    )
    layer_out = (residual + conditioning[3] * mixture).astype(jnp.bfloat16)
    return layer_out[None]


def solution(mesh):
    in_specs = (
        P("exp", "seq", None, None, None),
        P("exp", "seq", None),
        P("exp", None, None),
        P(),
        P("exp", "seq", None, None),
        P("exp", "seq", None),
        P("exp", None, "seq"),
        P("exp", "seq", None),
    )
    out_specs = P("exp", "seq", None)
    return jax.shard_map(
        per_device, mesh=mesh, in_specs=in_specs, out_specs=out_specs, check_vma=False
    )
```

profile of v0, /device:TPU:0, one launch (start us, length us, event | category | flops | bytes accessed | tf_op | source)
XLA Modules:
  0.0 145.9 jit_solution(4961994564393138970)
XLA Ops:
  6.5 3.0 %copy.26 = bf16[1,128,3,16,128]{4,1,2,0,3:T(8,128)(2,1)} copy(bf16[1,128,3,16,128]{4,3,2,1,0:T(8,128)(2,1)} %param.10) | data formatting | bytes 3145728 | tf_op args[0]
  9.5 6.3 %all-to-all-start = ((bf16[1,128,3,16,128]{4,1,2,0,3:T(8,128)(2,1)}), bf16[1,128,3,16,128]{4,1,2,0,3:T(8,128)(2,1)S(1)}, u32[]{:S(2)}, u32[]{:S(2)}) async-start(bf16[1,128,3,16,128]{4,1,2,0,3:T(8,128)(2,1)} %copy.26), calls=%async_computation | async-start | bytes 3145728 | tf_op jit(solution)/shard_map/all_to_all | solution.py:44
  15.9 37.0 %all-to-all-done = bf16[1,128,3,16,128]{4,1,2,0,3:T(8,128)(2,1)S(1)} async-done(((bf16[1,128,3,16,128]{4,1,2,0,3:T(8,128)(2,1)}), bf16[1,128,3,16,128]{4,1,2,0,3:T(8,128)(2,1)S(1)}, u32[]{:S(2)}, u32[]{:S(2)}) %all-to-all-start) | async-done | bytes 1572896 | tf_op jit(solution)/shard_map/all_to_all | solution.py:44
  53.0 6.3 %while.10 = (s32[]{:T(128)}, bf16[4,512,128]{2,1,0:T(8,128)(2,1)}, bf16[4,512,3,128]{3,1,2,0:T(8,128)(2,1)S(1)}, s32[]{:T(128)}) while((s32[]{:T(128)}, bf16[4,512,128]{2,1,0:T(8,128)(2,1)}, bf16[4,512,3,128]{3,1,2,0:T(8,128)(2,1)S(1)}, s32[]{:T(128)}) %tuple.32), condition=%wide.region_3.0_spmd, body=%wide.region_0.3_spmd.sunk | while | flops 136117248 | bytes 4467257 | solution.py:46
  53.1 0.3 fusion.68
  53.4 0.2 fusion.69
  53.6 1.0 fusion.70
  54.6 0.3 fusion.68
  55.0 0.2 fusion.69
  55.2 1.0 fusion.70
  56.2 0.3 fusion.68
  56.7 1.0 fusion.70
  57.8 0.3 fusion.68
  58.1 0.2 fusion.69
  58.3 1.0 fusion.70
  59.4 2.3 %copy.44 = bf16[4,512,128]{2,0,1:T(4,128)(2,1)} copy(bf16[4,512,128]{2,1,0:T(8,128)(2,1)} %get-tuple-element.37) | data formatting | bytes 1048576 | tf_op jit(solution)/shard_map/while | solution.py:46
  61.7 3.5 %all-to-all-start.1 = ((bf16[1,512,4,128]{3,2,0,1:T(4,128)(2,1)}), bf16[1,512,4,128]{3,2,0,1:T(4,128)(2,1)S(1)}, u32[]{:S(2)}, u32[]{:S(2)}) async-start(bf16[1,512,4,128]{3,2,0,1:T(4,128)(2,1)} %bitcast.96), calls=%async_computation.1 | async-start | bytes 1048576 | tf_op jit(solution)/shard_map/all_to_all | solution.py:48
  65.4 13.7 %all-to-all-done.1 = bf16[1,512,4,128]{3,2,0,1:T(4,128)(2,1)S(1)} async-done(((bf16[1,512,4,128]{3,2,0,1:T(4,128)(2,1)}), bf16[1,512,4,128]{3,2,0,1:T(4,128)(2,1)S(1)}, u32[]{:S(2)}, u32[]{:S(2)}) %all-to-all-start.1) | async-done | bytes 524320 | tf_op jit(solution)/shard_map/all_to_all | solution.py:48
  79.2 0.4 reshape.202
  79.7 1.4 reshape.203
  81.1 0.2 fusion.58
  81.3 0.3 multiply_reduce_fusion
  81.6 0.4 fusion.20
  82.3 0.4 convolution_convert_fusion.1
  82.7 8.5 %all_to_all.34 = bf16[8,2,2048]{2,1,0:T(2,128)(2,1)S(1)} all-to-all(bf16[8,2,2048]{2,1,0:T(2,128)(2,1)S(1)} %reshape.200), channel_id=1, replica_groups=mesh['exp'=8,'seq'=4] {'exp'}, dimensions={0} | all-to-all | bytes 131072 | tf_op jit(solution)/shard_map/all_to_all | solution.py:68
  91.3 14.4 %all_gather.3 = bf16[32,2,2048]{2,0,1:T(8,128)(2,1)S(1)} all-gather(bf16[8,2,2048]{2,0,1:T(8,128)(2,1)S(1)} %copy.31), channel_id=1, replica_groups=mesh['exp'=8,'seq'=4] {'seq'}, dimensions={0}, use_global_device_ids=true | all-gather | bytes 327680 | tf_op jit(solution)/shard_map/all_gather | solution.py:73
  105.7 5.1 %fusion.14 = bf16[2,4,8,2048]{3,2,1,0:T(8,128)(2,1)S(1)} fusion(bf16[1,1024,2048]{2,1,0:T(8,128)(2,1)} %param.17, bf16[32,2,2048]{2,0,1:T(8,128)(2,1)S(1)} %all_gather.3, bf16[1,2048,1024]{2,1,0:T(8,128)(2,1)} %param.16), kind=kOutput, calls=%fused_computation.21 | convolution fusion | flops 537591808 | bytes 8912896 | tf_op jit(solution)/shard_map/ncf,fd->ncd/dot_general | solution.py:79
  110.8 0.7 copy.37
  111.5 16.6 %reduce-scatter.4.cloned.1.call-done = bf16[8,4096]{1,0:T(8,128)(2,1)} async-done(((bf16[32,4096]{1,0:T(8,128)(2,1)}), bf16[8,4096]{1,0:T(8,128)(2,1)}) %reduce-scatter.4.cloned.1.call-update) | async-done | bytes 65552
  128.2 0.9 copy.32
  129.1 8.5 %all_to_all.35 = bf16[8,2,2048]{2,1,0:T(2,128)(2,1)S(1)} all-to-all(bf16[8,2,2048]{2,1,0:T(2,128)(2,1)S(1)} %copy.32), channel_id=1, replica_groups=mesh['exp'=8,'seq'=4] {'exp'}, dimensions={0} | all-to-all | bytes 131072 | tf_op jit(solution)/shard_map/all_to_all | solution.py:86
  137.6 1.5 %fusion.10 = bf16[1,128,2048]{2,1,0:T(8,128)(2,1)} fusion(f32[2048]{0:T(1024)S(1)} %bitcast.117, bf16[8,2,2048]{2,1,0:T(2,128)(2,1)S(1)} %all_to_all.35, f32[8,2,128]{2,1,0:T(2,128)S(1)} %get-tuple-element.44, f32[128,2048]{1,0:T(8,128)S(1)} %reshape.202, f32[2048]{0:T(1024)S(1)} %bitcast.115, bf16[1,128,2048]{2,1,0:T(8,128)(2,1)S(1)} %copy-done.1), kind=kOutput, calls=%fused_computation.19 | convolution fusion | flops 51904512 | bytes 2187264 | tf_op jit(solution)/shard_map/ect,ecd->td/dot_general | solution.py:88
  (32 shorter events, 1.2 us)
Async XLA Ops:
  6.5 75.1 %copy-start = (bf16[2048,8]{0,1:T(8,128)(2,1)S(1)}, bf16[2048,8]{0,1:T(8,128)(2,1)}, u32[]{:S(2)}) copy-start(bf16[2048,8]{0,1:T(8,128)(2,1)} %param.13) | copy-start | bytes 98308
  9.5 43.3 %all-to-all-start = ((bf16[1,128,3,16,128]{4,1,2,0,3:T(8,128)(2,1)}), bf16[1,128,3,16,128]{4,1,2,0,3:T(8,128)(2,1)S(1)}, u32[]{:S(2)}, u32[]{:S(2)}) async-start(bf16[1,128,3,16,128]{4,1,2,0,3:T(8,128)(2,1)} %copy.26), calls=%async_computation | async-start | bytes 3145728 | tf_op jit(solution)/shard_map/all_to_all | solution.py:44
  53.0 12.2 %copy-start.4 = (s32[1,1,8,2]{2,3,1,0:T(2,128)S(1)}, s32[1,1,8,2]{2,3,1,0:T(2,128)}, u32[]{:S(2)}) copy-start(s32[1,1,8,2]{2,3,1,0:T(2,128)} %param.14) | copy-start | bytes 196
  53.0 12.3 %copy-start.5 = (s32[1,1,8]{2,1,0:T(1,128)S(1)}, s32[1,1,8]{2,1,0:T(1,128)}, u32[]{:S(2)}) copy-start(s32[1,1,8]{2,1,0:T(1,128)} %param.15) | copy-start | bytes 100
  53.0 12.4 %copy-start.3 = (f32[1,4,2048]{2,1,0:T(4,128)S(1)}, f32[1,4,2048]{2,1,0:T(4,128)}, u32[]{:S(2)}) copy-start(f32[1,4,2048]{2,1,0:T(4,128)} %param.12) | copy-start | bytes 98308
  59.4 21.7 %copy-start.1 = (bf16[1,128,2048]{2,1,0:T(8,128)(2,1)S(1)}, bf16[1,128,2048]{2,1,0:T(8,128)(2,1)}, u32[]{:S(2)}) copy-start(bf16[1,128,2048]{2,1,0:T(8,128)(2,1)} %param.11) | copy-start | bytes 1572868
  61.7 17.4 %all-to-all-start.1 = ((bf16[1,512,4,128]{3,2,0,1:T(4,128)(2,1)}), bf16[1,512,4,128]{3,2,0,1:T(4,128)(2,1)S(1)}, u32[]{:S(2)}, u32[]{:S(2)}) async-start(bf16[1,512,4,128]{3,2,0,1:T(4,128)(2,1)} %bitcast.96), calls=%async_computation.1 | async-start | bytes 1048576 | tf_op jit(solution)/shard_map/all_to_all | solution.py:48
  65.1 63.0 %reduce-scatter.4.cloned.1.call-start = ((), (), s32[]{:S(2)}) async-start(), calls=%async_computation.5 | async-start | bytes 327680
  81.1 1.2 copy-start.2
Sparse Core Ops, SparseCore 0:
  111.6 16.4 reduce-scatter.3
where the time goes:
time: 146 us
  waiting for transfers between devices  67.3 us (46%)
  blocking collectives  31.4 us (22%)
  between operations  13.5 us (9%)
  matrix products  12.8 us (9%)
  starting transfers between devices  9.83 us (7%)
  local copies, waits for them, and re-layouts  9.38 us (6%)
  other arithmetic  1.65 us (1%)
    all_to_all x1, waiting for transfers between devices, per_device(): lax.all_to_all(projected, 'seq', split_axis=3, concat_axis=1, tiled=True)  37 us
    unnamed x2, waiting for transfers between devices  16.7 us
    all_gather x1, blocking collectives, per_device(): lax.all_gather(arrived, 'seq', axis=0, tiled=True)  14.4 us
    all_to_all x1, waiting for transfers between devices, per_device(): lax.all_to_all(attended, 'seq', split_axis=1, concat_axis=2, tiled=True)  13.7 us
    all_to_all x1, blocking collectives, per_device(): lax.all_to_all(dispatch_rows, 'exp', split_axis=0, concat_axis=0, tiled=T...  8.54 us
    all_to_all x1, blocking collectives, per_device(): lax.all_to_all(summed, 'exp', split_axis=0, concat_axis=0, tiled=True)  8.51 us
    all_to_all x1, starting transfers between devices, per_device(): lax.all_to_all(projected, 'seq', split_axis=3, concat_axis=1, tiled=True)  6.32 us
    dot_general x1, matrix products, per_device(): jnp.einsum('ncf,fd->ncd', hidden, expert_out, preferred_element_type=jnp....  5.1 us
  transfers between devices with their start and end apart: 3, of which 3 were waited for; matrix products, arithmetic and copies ran while one was open for 0% of the time, Pallas kernels for 0%

commit v1 on v0

v1 whole, which is shorter than its diff:
```python
import functools
import math

import jax
import jax.numpy as jnp
from jax import lax
from jax.experimental import pallas as pl
from jax.experimental.pallas import tpu as pltpu
from jax.sharding import PartitionSpec as P

epsilon_norm = 1e-06
MESH = pl.DeviceIdType.MESH
BF = jnp.bfloat16
F32 = jnp.float32


def block_kernel(
    n_exp,
    n_seq,
    heads,
    cap,
    picked_ref,
    counts_ref,
    proj_hbm,
    hidden_hbm,
    mod_hbm,
    router_hbm,
    win_hbm,
    wout_hbm,
    out_ref,
    proj,
    hidden_in,
    mod,
    router,
    win,
    wout,
    wide,
    qkv_out,
    qkv_in,
    att_out,
    att_in,
    resid,
    stage,
    rows_out,
    rows_in,
    rows_x,
    ret_out,
    ret_in,
    rows_e,
    load_sem,
    qkv_send,
    qkv_recv,
    qkv_own,
    att_send,
    att_recv,
    att_own,
    row_send,
    row_recv,
    ret_send,
    ret_recv,
):
    me_e = lax.axis_index("exp")
    me_s = lax.axis_index("seq")
    devices = n_exp * n_seq
    toks = hidden_in.shape[0]
    width = hidden_in.shape[1]
    head = proj.shape[1]
    local_heads = heads // n_seq
    length = toks * n_seq
    slots = n_exp * cap
    pieces = width // head
    me = me_e * n_seq + me_s

    def peer_of(d):
        return (
            lax.rem(me_e + d // n_seq, n_exp),
            lax.rem(me_s + lax.rem(d, n_seq), n_seq),
        )

    barrier = pltpu.get_barrier_semaphore()

    def greet(d, carry):
        pl.semaphore_signal(barrier, inc=1, device_id=peer_of(d), device_id_type=MESH)
        return carry

    lax.fori_loop(1, devices, greet, 0)

    loads = [
        pltpu.make_async_copy(src, dst, load_sem.at[i])
        for i, (src, dst) in enumerate(
            (
                (proj_hbm, proj),
                (hidden_hbm, hidden_in),
                (mod_hbm, mod),
                (router_hbm, router),
                (win_hbm, win),
                (wout_hbm, wout),
            )
        )
    ]
    for load in loads:
        load.start()

    loads[0].wait()
    wide[...] = proj[...].astype(F32)
    qkv_copies = []
    for j in range(local_heads):
        for s in range(n_seq):
            for c in range(3):
                first = c * heads + s * local_heads + j
                qkv_out[j, s, c] = wide[pl.ds(first, toks, stride=3 * heads), :].astype(BF)
        if j == 0:
            pl.semaphore_wait(barrier, devices - 1)
        sent = []
        for d in range(1, n_seq):
            peer = lax.rem(me_s + d, n_seq)
            copy = pltpu.make_async_remote_copy(
                src_ref=qkv_out.at[j, peer],
                dst_ref=qkv_in.at[j, :, me_s],
                send_sem=qkv_send.at[j, d],
                recv_sem=qkv_recv.at[j, d],
                device_id=(me_e, peer),
                device_id_type=MESH,
            )
            copy.start()
            sent.append(copy)
        own = pltpu.make_async_copy(qkv_out.at[j, me_s], qkv_in.at[j, :, me_s], qkv_own.at[j])
        own.start()
        qkv_copies.append((sent, own))

    row_ids = lax.broadcasted_iota(jnp.int32, (slots, toks), 0)
    col_ids = lax.broadcasted_iota(jnp.int32, (toks, slots), 1)
    row_pos = jnp.full((slots, toks), -1, jnp.int32)
    col_pos = jnp.full((toks, slots), -1, jnp.int32)
    for e in range(n_exp):
        for c in range(cap):
            pos = jnp.where(c < counts_ref[0, e], picked_ref[e, c] - me_s * toks, -1)
            row_pos = jnp.where(row_ids == e * cap + c, pos, row_pos)
            col_pos = jnp.where(col_ids == e * cap + c, pos, col_pos)
    pick_rows = row_pos == lax.broadcasted_iota(jnp.int32, (slots, toks), 1)
    pick_cols = col_pos == lax.broadcasted_iota(jnp.int32, (toks, slots), 0)
    pick_rows = jnp.where(pick_rows, 1.0, 0.0).astype(BF)
    pick_cols = jnp.where(pick_cols, 1.0, 0.0)

    score_scale = 1.0 / math.sqrt(head)
    group = min(512 // toks, n_seq)
    att_copies = []
    for j in range(local_heads):
        sent, own = qkv_copies[j]
        own.wait()
        for copy in sent:
            copy.wait_recv()

        def attend(b, carry, j=j):
            at = pl.ds(b * group, group)
            queries = qkv_in[j, 0, at].reshape(group * toks, head)
            keys = qkv_in[j, 1].reshape(length, head)
            values = qkv_in[j, 2].reshape(length, head)
            scores = lax.dot_general(
                queries, keys, (((1,), (1,)), ((), ())), preferred_element_type=F32
            )
            scores = scores * score_scale
            weights = jnp.exp(scores - jnp.max(scores, axis=-1, keepdims=True))
            weights = weights * (1.0 / jnp.sum(weights, axis=-1, keepdims=True))
            mixed = jnp.dot(weights.astype(BF), values, preferred_element_type=F32)
            att_out[j, at] = mixed.astype(BF).reshape(group, toks, head)
            return carry

        if n_seq == group:
            attend(0, 0)
        else:
            lax.fori_loop(0, n_seq // group, attend, 0)
        sent = []
        for d in range(1, n_seq):
            peer = lax.rem(me_s + d, n_seq)
            copy = pltpu.make_async_remote_copy(
                src_ref=att_out.at[j, peer],
                dst_ref=att_in.at[j, me_s],
                send_sem=att_send.at[j, d],
                recv_sem=att_recv.at[j, d],
                device_id=(me_e, peer),
                device_id_type=MESH,
            )
            copy.start()
            sent.append(copy)
        own = pltpu.make_async_copy(att_out.at[j, me_s], att_in.at[j, me_s], att_own.at[j])
        own.start()
        att_copies.append((sent, own))

    for load in loads[1:]:
        load.wait()
    for j in range(local_heads):
        sent, own = att_copies[j]
        own.wait()
        for copy in sent:
            copy.wait_recv()
        for s in range(n_seq):
            first = (s * local_heads + j) * head
            at = slice(first, first + head)
            resid[:, at] = hidden_in[:, at].astype(F32) + mod[0:1, at] * att_in[j, s].astype(F32)

    residual = resid[...]
    centred = residual - jnp.mean(residual, axis=-1, keepdims=True)
    variance = jnp.mean(centred * centred, axis=-1, keepdims=True)
    normed = centred * lax.rsqrt(variance + epsilon_norm)
    modulated = (normed * (1.0 + mod[2:3, :]) + mod[1:2, :]).astype(BF)

    picked_rows = jnp.dot(pick_rows, modulated, preferred_element_type=F32)
    for k in range(pieces):
        stage[pl.ds(k, slots, stride=pieces), :] = picked_rows[:, k * head : (k + 1) * head]
    rows_out[...] = stage[0 : slots * pieces, :].reshape(rows_out.shape).astype(BF)

    def send_rows(d, carry):
        peer_e, peer_s = peer_of(d)
        pltpu.make_async_remote_copy(
            src_ref=rows_out.at[peer_e],
            dst_ref=rows_in.at[me],
            send_sem=row_send,
            recv_sem=row_recv,
            device_id=(peer_e, peer_s),
            device_id_type=MESH,
        ).start()
        return carry

    lax.fori_loop(1, devices, send_rows, 0)
    pltpu.make_async_copy(rows_out.at[me_e], rows_in.at[me], row_recv).start()

    gates = jax.nn.sigmoid(jnp.dot(modulated, router[...], preferred_element_type=F32))
    gate_cols = jnp.zeros((toks, slots), F32)
    for e in range(n_exp):
        gate_cols = jnp.where(col_ids // cap == e, gates[:, e : e + 1], gate_cols)
    gate_cols = gate_cols * pick_cols
    gate_high = gate_cols.astype(BF)
    gate_low = (gate_cols - gate_high.astype(F32)).astype(BF)

    pltpu.make_async_copy(rows_in, rows_in, row_recv).wait()

    block = rows_x.shape[0]
    sources = block // cap

    def apply_expert(b, carry):
        at = pl.ds(b * sources, sources)
        stage[0 : block * pieces, :] = rows_in[at].astype(F32).reshape(block * pieces, head)
        for k in range(pieces):
            rows_x[:, k * head : (k + 1) * head] = stage[
                pl.ds(k, block, stride=pieces), :
            ].astype(BF)
        product = jnp.dot(rows_x[...], win[...], preferred_element_type=F32)
        units = jax.nn.gelu(product, approximate=True).astype(BF)
        partial = jnp.dot(units, wout[...], preferred_element_type=F32)
        for k in range(pieces):
            stage[pl.ds(k, block, stride=pieces), :] = partial[:, k * head : (k + 1) * head]
        ret_out[at] = stage[0 : block * pieces, :].reshape(sources, cap * pieces, head).astype(BF)
        return carry

    if devices == sources:
        apply_expert(0, 0)
    else:
        lax.fori_loop(0, devices // sources, apply_expert, 0)

    def send_back(d, carry):
        peer_e, peer_s = peer_of(d)
        pltpu.make_async_remote_copy(
            src_ref=ret_out.at[peer_e * n_seq + peer_s],
            dst_ref=ret_in.at[me],
            send_sem=ret_send,
            recv_sem=ret_recv,
            device_id=(peer_e, peer_s),
            device_id_type=MESH,
        ).start()
        return carry

    lax.fori_loop(1, devices, send_back, 0)
    pltpu.make_async_copy(ret_out.at[me], ret_in.at[me], ret_recv).start()

    for sent, _ in qkv_copies + att_copies:
        for copy in sent:
            copy.wait_send()
    others = rows_in.at[pl.ds(0, devices - 1)]
    pltpu.make_async_copy(others, others, row_send).wait()

    pltpu.make_async_copy(ret_in, ret_in, ret_recv).wait()
    for e in range(n_exp):
        summed = jnp.sum(ret_in[e * n_seq : (e + 1) * n_seq].astype(F32), axis=0)
        stage[e * cap * pieces : (e + 1) * cap * pieces, :] = summed
    for k in range(pieces):
        rows_e[:, k * head : (k + 1) * head] = stage[pl.ds(k, slots, stride=pieces), :].astype(BF)
    expert_rows = rows_e[...]
    mixture = jnp.dot(gate_high, expert_rows, preferred_element_type=F32) + jnp.dot(
        gate_low, expert_rows, preferred_element_type=F32
    )
    out_ref[...] = (resid[...] + mod[3:4, :] * mixture).astype(BF)

    others = ret_in.at[pl.ds(0, devices - 1)]
    pltpu.make_async_copy(others, others, ret_send).wait()


def per_device(
    n_exp, n_seq, projected, hidden_in, modulation, w_router, picked, counts, weight_in, weight_out
):
    _, toks, three, heads, head = projected.shape
    width = hidden_in.shape[2]
    units = weight_in.shape[2]
    experts = w_router.shape[1]
    cap = picked.shape[3]
    devices = n_exp * n_seq
    slots = experts * cap
    pieces = width // head
    local_heads = heads // n_seq
    block = min(64, devices * cap)
    dma = pltpu.SemaphoreType.DMA
    anywhere = pl.BlockSpec(memory_space=pl.ANY)
    scalars = pl.BlockSpec(memory_space=pltpu.SMEM)
    rows = toks * three * heads
    flops = (
        4 * local_heads * (toks * n_seq) ** 2 * head + 4 * devices * cap * width * units
    )
    out = pl.pallas_call(
        functools.partial(block_kernel, n_exp, n_seq, heads, cap),
        out_shape=jax.ShapeDtypeStruct((toks, width), BF),
        in_specs=[scalars] * 2 + [anywhere] * 6,
        out_specs=pl.BlockSpec(memory_space=pltpu.VMEM),
        scratch_shapes=[
            pltpu.VMEM((rows, head), BF),
            pltpu.VMEM((toks, width), BF),
            pltpu.VMEM((4, width), F32),
            pltpu.VMEM((width, experts), BF),
            pltpu.VMEM((width, units), BF),
            pltpu.VMEM((units, width), BF),
            pltpu.VMEM((rows, head), F32),
            pltpu.VMEM((local_heads, n_seq, three, toks, head), BF),
            pltpu.VMEM((local_heads, three, n_seq, toks, head), BF),
            pltpu.VMEM((local_heads, n_seq, toks, head), BF),
            pltpu.VMEM((local_heads, n_seq, toks, head), BF),
            pltpu.VMEM((toks, width), F32),
            pltpu.VMEM((max(block, slots) * pieces, head), F32),
            pltpu.VMEM((experts, cap * pieces, head), BF),
            pltpu.VMEM((devices, cap * pieces, head), BF),
            pltpu.VMEM((block, width), BF),
            pltpu.VMEM((devices, cap * pieces, head), BF),
            pltpu.VMEM((devices, cap * pieces, head), BF),
            pltpu.VMEM((slots, width), BF),
            dma((6,)),
            dma((local_heads, n_seq)),
            dma((local_heads, n_seq)),
            dma((local_heads,)),
            dma((local_heads, n_seq)),
            dma((local_heads, n_seq)),
            dma((local_heads,)),
            dma,
            dma,
            dma,
            dma,
        ],
        compiler_params=pltpu.CompilerParams(
            collective_id=0, has_side_effects=True, vmem_limit_bytes=56 * 1024 * 1024
        ),
        cost_estimate=pl.CostEstimate(
            flops=flops, bytes_accessed=4 * width * units, transcendentals=0
        ),
    )(
        picked.reshape(experts, cap),
        counts.reshape(1, experts),
        projected.reshape(rows, head),
        hidden_in[0],
        modulation[0],
        w_router,
        weight_in[0],
        weight_out[0],
    )
    return out[None]


def solution(mesh):
    in_specs = (
        P("exp", "seq", None, None, None),
        P("exp", "seq", None),
        P("exp", None, None),
        P(),
        P("exp", "seq", None, None),
        P("exp", "seq", None),
        P("exp", None, "seq"),
        P("exp", "seq", None),
    )
    out_specs = P("exp", "seq", None)
    return jax.shard_map(
        functools.partial(per_device, mesh.shape["exp"], mesh.shape["seq"]),
        mesh=mesh,
        in_specs=in_specs,
        out_specs=out_specs,
        check_vma=False,
    )
```

time: 146 us -> 79.5 us (0.54)
  Pallas kernels: 0 us -> 74.2 us
  waiting for transfers between devices: 67.3 us -> 0 us
  blocking collectives: 31.4 us -> 0 us
  between operations: 13.5 us -> 0.01 us
  matrix products: 12.8 us -> 0 us
  starting transfers between devices: 9.83 us -> 0 us
  local copies, waits for them, and re-layouts: 9.38 us -> 4.99 us
  other arithmetic: 1.65 us -> 0 us
    pallas_call x0 -> x1, Pallas kernels: none -> 74.2 us  [per_device(): pl.pallas_call(functools.partial(block_kernel, n_exp, n_seq, heads, cap),...]
    all_to_all x2 -> x0, waiting for transfers between devices: 50.7 us -> none  [the longest x1 37 us: per_device(): lax.all_to_all(projected, 'seq', split_axis=3, concat_axis=1, tiled=True)]
    all_to_all x2 -> x0, blocking collectives: 17.1 us -> none  [the longest x1 8.54 us: per_device(): lax.all_to_all(dispatch_rows, 'exp', split_axis=0, concat_axis=0, tiled=T...]
    unnamed x2 -> x0, waiting for transfers between devices: 16.7 us -> none
    all_gather x1 -> x0, blocking collectives: 14.4 us -> none  [per_device(): lax.all_gather(arrived, 'seq', axis=0, tiled=True)]
    dot_general x12 -> x0, matrix products: 12.8 us -> none  [the longest x1 5.1 us: per_device(): jnp.einsum('ncf,fd->ncd', hidden, expert_out, preferred_element_type=jnp....]
    all_to_all x2 -> x0, starting transfers between devices: 9.79 us -> none  [the longest x1 6.32 us: per_device(): lax.all_to_all(projected, 'seq', split_axis=3, concat_axis=1, tiled=True)]
    while x1 -> x0, local copies, waits for them, and re-layouts: 2.3 us -> none  [per_device(): attended = lax.map(head_attention, per_head)]
  transfers between devices with their start and end apart: 3 -> 0, of which waited for: 3 -> 0; matrix products, arithmetic and copies ran while one was open for 0% -> 0% of each run, Pallas kernels for 0% -> 0%
where the time goes in v1:
time: 79.5 us; the launch traced here: 79.2 us
  Pallas kernels  74.2 us (93%)
  local copies, waits for them, and re-layouts  4.99 us (6%)
    pallas_call x1, Pallas kernels, per_device(): pl.pallas_call(functools.partial(block_kernel, n_exp, n_seq, heads, cap),...  74.2 us
    unnamed x2, local copies, waits for them, and re-layouts  3.64 us

profile of v1, /device:TPU:0, one launch (start us, length us, event | category | flops | bytes accessed | tf_op | source)
XLA Modules:
  0.0 79.2 jit_solution(8066512943208991079)
XLA Ops:
  0.0 1.3 %copy.9.picked_ref = s32[8,2]{1,0:T(8,128)} copy(s32[8,2]{0,1:T(2,128)} %bitcast.14) | data formatting | bytes 128 | tf_op jit(solution)/shard_map/reshape | solution.py:362
  1.3 1.8 %copy.10.router_hbm = bf16[2048,8]{1,0:T(8,128)(2,1)} copy(bf16[2048,8]{0,1:T(8,128)(2,1)} %param.11) | data formatting | bytes 65536 | tf_op args[3]
  3.1 74.2 %shard_map.82 = bf16[128,2048]{1,0:T(8,128)(2,1)} custom-call(s32[8,2]{1,0:T(8,128)} %copy.9.picked_ref, s32[1,8]{1,0:T(1,128)} %bitcast.15, bf16[6144,128]{1,0:T(8,128)(2,1)} %bitcast.11, bf16[128,2048]{1,0:T(8,128)(2,1)} %bitcast.12, f32[4,2048]{1,0:T(4,128)} %bitcast.13, bf16[2048,8]{1,0:T(8,128)(2,1)} %copy.10.router_hbm, bf16[2048,1024]{1,0:T(8,128)(2,1)} %bitcast.8, ...), custom_call_target="tpu_custom_call" | custom-call | flops 1073741824 | bytes 8388608 | tf_op jit(solution)/shard_map/pallas_call | solution.py:318
  77.3 1.9 %copy.12 = bf16[1,128,2048]{2,1,0:T(8,128)(2,1)} copy(bf16[1,128,2048]{2,1,0:T(8,128)(2,1)} %bitcast.10) | data formatting | bytes 1048576

commit v2 on v1

--- a/solution.py
+++ b/solution.py
@@ -71,19 +71,25 @@
     pieces = width // head
     me = me_e * n_seq + me_s
 
-    def peer_of(d):
-        return (
-            lax.rem(me_e + d // n_seq, n_exp),
-            lax.rem(me_s + lax.rem(d, n_seq), n_seq),
-        )
+    offsets = list(range(n_seq // 2, n_seq)) + list(range(n_seq // 2 - 1, -1, -1))
+
+    def to_all(send):
+        for ds in offsets:
+
+            def step(de, carry, ds=ds):
+                send(lax.rem(me_e + de, n_exp), lax.rem(me_s + ds, n_seq))
+                return carry
+
+            lax.fori_loop(0 if ds else 1, n_exp, step, 0)
 
     barrier = pltpu.get_barrier_semaphore()
-
-    def greet(d, carry):
-        pl.semaphore_signal(barrier, inc=1, device_id=peer_of(d), device_id_type=MESH)
-        return carry
-
-    lax.fori_loop(1, devices, greet, 0)
+    greeted = n_seq - 1 + n_exp - 1
+    for d in range(1, n_seq):
+        peer = (me_e, lax.rem(me_s + d, n_seq))
+        pl.semaphore_signal(barrier, inc=1, device_id=peer, device_id_type=MESH)
+    for d in range(1, n_exp):
+        peer = (lax.rem(me_e + d, n_exp), me_s)
+        pl.semaphore_signal(barrier, inc=1, device_id=peer, device_id_type=MESH)
 
     loads = [
         pltpu.make_async_copy(src, dst, load_sem.at[i])
@@ -110,7 +116,7 @@
                 first = c * heads + s * local_heads + j
                 qkv_out[j, s, c] = wide[pl.ds(first, toks, stride=3 * heads), :].astype(BF)
         if j == 0:
-            pl.semaphore_wait(barrier, devices - 1)
+            pl.semaphore_wait(barrier, greeted)
         sent = []
         for d in range(1, n_seq):
             peer = lax.rem(me_s + d, n_seq)
@@ -134,7 +140,7 @@
     col_pos = jnp.full((toks, slots), -1, jnp.int32)
     for e in range(n_exp):
         for c in range(cap):
-            pos = jnp.where(c < counts_ref[0, e], picked_ref[e, c] - me_s * toks, -1)
+            pos = jnp.where(c < counts_ref[0, e], picked_ref[c, e] - me_s * toks, -1)
             row_pos = jnp.where(row_ids == e * cap + c, pos, row_pos)
             col_pos = jnp.where(col_ids == e * cap + c, pos, col_pos)
     pick_rows = row_pos == lax.broadcasted_iota(jnp.int32, (slots, toks), 1)
@@ -210,8 +216,7 @@
         stage[pl.ds(k, slots, stride=pieces), :] = picked_rows[:, k * head : (k + 1) * head]
     rows_out[...] = stage[0 : slots * pieces, :].reshape(rows_out.shape).astype(BF)
 
-    def send_rows(d, carry):
-        peer_e, peer_s = peer_of(d)
+    def send_rows(peer_e, peer_s):
         pltpu.make_async_remote_copy(
             src_ref=rows_out.at[peer_e],
             dst_ref=rows_in.at[me],
@@ -220,12 +225,15 @@
             device_id=(peer_e, peer_s),
             device_id_type=MESH,
         ).start()
-        return carry
-
-    lax.fori_loop(1, devices, send_rows, 0)
+
+    to_all(send_rows)
     pltpu.make_async_copy(rows_out.at[me_e], rows_in.at[me], row_recv).start()
 
-    gates = jax.nn.sigmoid(jnp.dot(modulated, router[...], preferred_element_type=F32))
+    gates = jax.nn.sigmoid(
+        lax.dot_general(
+            modulated, router[...], (((1,), (1,)), ((), ())), preferred_element_type=F32
+        )
+    )
     gate_cols = jnp.zeros((toks, slots), F32)
     for e in range(n_exp):
         gate_cols = jnp.where(col_ids // cap == e, gates[:, e : e + 1], gate_cols)
@@ -258,8 +266,7 @@
     else:
         lax.fori_loop(0, devices // sources, apply_expert, 0)
 
-    def send_back(d, carry):
-        peer_e, peer_s = peer_of(d)
+    def send_back(peer_e, peer_s):
         pltpu.make_async_remote_copy(
             src_ref=ret_out.at[peer_e * n_seq + peer_s],
             dst_ref=ret_in.at[me],
@@ -268,9 +275,8 @@
             device_id=(peer_e, peer_s),
             device_id_type=MESH,
         ).start()
-        return carry
-
-    lax.fori_loop(1, devices, send_back, 0)
+
+    to_all(send_back)
     pltpu.make_async_copy(ret_out.at[me], ret_in.at[me], ret_recv).start()
 
     for sent, _ in qkv_copies + att_copies:
@@ -324,7 +330,7 @@
             pltpu.VMEM((rows, head), BF),
             pltpu.VMEM((toks, width), BF),
             pltpu.VMEM((4, width), F32),
-            pltpu.VMEM((width, experts), BF),
+            pltpu.VMEM((experts, width), BF),
             pltpu.VMEM((width, units), BF),
             pltpu.VMEM((units, width), BF),
             pltpu.VMEM((rows, head), F32),
@@ -359,12 +365,12 @@
             flops=flops, bytes_accessed=4 * width * units, transcendentals=0
         ),
     )(
-        picked.reshape(experts, cap),
+        picked.reshape(experts, cap).T,
         counts.reshape(1, experts),
         projected.reshape(rows, head),
         hidden_in[0],
         modulation[0],
-        w_router,
+        w_router.T,
         weight_in[0],
         weight_out[0],
     )

time: 79.5 us -> 73.7 us (0.927)
  local copies, waits for them, and re-layouts: 4.99 us -> 1.88 us
  Pallas kernels: 74.2 us -> 71.6 us
    pallas_call x1, Pallas kernels: 74.2 us -> 71.6 us  [per_device(): pl.pallas_call(functools.partial(block_kernel, n_exp, n_seq, heads, cap),...]
    unnamed x2 -> x1, local copies, waits for them, and re-layouts: 3.64 us -> 1.88 us
    reshape x1 -> x0, local copies, waits for them, and re-layouts: 1.34 us -> none  [per_device(): picked.reshape(experts, cap)]
where the time goes in v2:
time: 73.7 us; the launch traced here: 73.5 us
  Pallas kernels  71.6 us (97%)
  local copies, waits for them, and re-layouts  1.88 us (3%)
    pallas_call x1, Pallas kernels, per_device(): pl.pallas_call(functools.partial(block_kernel, n_exp, n_seq, heads, cap),...  71.6 us
    unnamed x1, local copies, waits for them, and re-layouts  1.88 us

profile of v2, /device:TPU:0, one launch (start us, length us, event | category | flops | bytes accessed | tf_op | source)
XLA Modules:
  0.0 73.5 jit_solution(1982372303631610689)
XLA Ops:
  0.0 71.6 %shard_map.82 = bf16[128,2048]{1,0:T(8,128)(2,1)} custom-call(s32[2,8]{1,0:T(2,128)} %bitcast.18, s32[1,8]{1,0:T(1,128)} %bitcast.19, bf16[6144,128]{1,0:T(8,128)(2,1)} %bitcast.14, bf16[128,2048]{1,0:T(8,128)(2,1)} %bitcast.15, f32[4,2048]{1,0:T(4,128)} %bitcast.16, bf16[8,2048]{1,0:T(8,128)(2,1)} %bitcast.17, bf16[2048,1024]{1,0:T(8,128)(2,1)} %bitcast.11, ...), custom_call_target="tpu_custom_call" | custom-call | flops 1073741824 | bytes 8388608 | tf_op jit(solution)/shard_map/pallas_call | solution.py:324
  71.6 1.9 %copy.10 = bf16[1,128,2048]{2,1,0:T(8,128)(2,1)} copy(bf16[1,128,2048]{2,1,0:T(8,128)(2,1)} %bitcast.13) | data formatting | bytes 1048576

commit v3 on v2

--- a/solution.py
+++ b/solution.py
@@ -19,8 +19,8 @@
     n_seq,
     heads,
     cap,
-    picked_ref,
-    counts_ref,
+    picked_hbm,
+    counts_hbm,
     proj_hbm,
     hidden_hbm,
     mod_hbm,
@@ -28,6 +28,8 @@
     win_hbm,
     wout_hbm,
     out_ref,
+    picked_ref,
+    counts_ref,
     proj,
     hidden_in,
     mod,
@@ -101,6 +103,8 @@
                 (router_hbm, router),
                 (win_hbm, win),
                 (wout_hbm, wout),
+                (picked_hbm, picked_ref),
+                (counts_hbm, counts_ref),
             )
         )
     ]
@@ -134,6 +138,9 @@
         own.start()
         qkv_copies.append((sent, own))
 
+    for load in loads[6:]:
+        load.wait()
+
     row_ids = lax.broadcasted_iota(jnp.int32, (slots, toks), 0)
     col_ids = lax.broadcasted_iota(jnp.int32, (toks, slots), 1)
     row_pos = jnp.full((slots, toks), -1, jnp.int32)
@@ -151,31 +158,8 @@
     score_scale = 1.0 / math.sqrt(head)
     group = min(512 // toks, n_seq)
     att_copies = []
-    for j in range(local_heads):
-        sent, own = qkv_copies[j]
-        own.wait()
-        for copy in sent:
-            copy.wait_recv()
-
-        def attend(b, carry, j=j):
-            at = pl.ds(b * group, group)
-            queries = qkv_in[j, 0, at].reshape(group * toks, head)
-            keys = qkv_in[j, 1].reshape(length, head)
-            values = qkv_in[j, 2].reshape(length, head)
-            scores = lax.dot_general(
-                queries, keys, (((1,), (1,)), ((), ())), preferred_element_type=F32
-            )
-            scores = scores * score_scale
-            weights = jnp.exp(scores - jnp.max(scores, axis=-1, keepdims=True))
-            weights = weights * (1.0 / jnp.sum(weights, axis=-1, keepdims=True))
-            mixed = jnp.dot(weights.astype(BF), values, preferred_element_type=F32)
-            att_out[j, at] = mixed.astype(BF).reshape(group, toks, head)
-            return carry
-
-        if n_seq == group:
-            attend(0, 0)
-        else:
-            lax.fori_loop(0, n_seq // group, attend, 0)
+
+    def send_back_heads(j):
         sent = []
         for d in range(1, n_seq):
             peer = lax.rem(me_s + d, n_seq)
@@ -193,7 +177,39 @@
         own.start()
         att_copies.append((sent, own))
 
-    for load in loads[1:]:
+    for j in range(local_heads):
+        sent, own = qkv_copies[j]
+        if 0 < j == local_heads - 1:
+            for copy in sent:
+                copy.wait_send()
+            for earlier in range(j):
+                send_back_heads(earlier)
+        own.wait()
+        for copy in sent:
+            copy.wait_recv()
+
+        def attend(b, carry, j=j):
+            at = pl.ds(b * group, group)
+            queries = qkv_in[j, 0, at].reshape(group * toks, head)
+            keys = qkv_in[j, 1].reshape(length, head)
+            values = qkv_in[j, 2].reshape(length, head)
+            scores = lax.dot_general(
+                queries, keys, (((1,), (1,)), ((), ())), preferred_element_type=F32
+            )
+            scores = scores * score_scale
+            weights = jnp.exp(scores - jnp.max(scores, axis=-1, keepdims=True))
+            weights = weights * (1.0 / jnp.sum(weights, axis=-1, keepdims=True))
+            mixed = jnp.dot(weights.astype(BF), values, preferred_element_type=F32)
+            att_out[j, at] = mixed.astype(BF).reshape(group, toks, head)
+            return carry
+
+        if n_seq == group:
+            attend(0, 0)
+        else:
+            lax.fori_loop(0, n_seq // group, attend, 0)
+    send_back_heads(local_heads - 1)
+
+    for load in loads[1:6]:
         load.wait()
     for j in range(local_heads):
         sent, own = att_copies[j]
@@ -211,23 +227,35 @@
     normed = centred * lax.rsqrt(variance + epsilon_norm)
     modulated = (normed * (1.0 + mod[2:3, :]) + mod[1:2, :]).astype(BF)
 
+    parts = rows_in.shape[0]
+    depth = pieces // parts
+
+    def columns(part, k):
+        return slice((part * depth + k) * head, (part * depth + k + 1) * head)
+
+    def part_columns(part):
+        return slice(part * depth * head, (part + 1) * depth * head)
+
     picked_rows = jnp.dot(pick_rows, modulated, preferred_element_type=F32)
-    for k in range(pieces):
-        stage[pl.ds(k, slots, stride=pieces), :] = picked_rows[:, k * head : (k + 1) * head]
-    rows_out[...] = stage[0 : slots * pieces, :].reshape(rows_out.shape).astype(BF)
-
-    def send_rows(peer_e, peer_s):
-        pltpu.make_async_remote_copy(
-            src_ref=rows_out.at[peer_e],
-            dst_ref=rows_in.at[me],
-            send_sem=row_send,
-            recv_sem=row_recv,
-            device_id=(peer_e, peer_s),
-            device_id_type=MESH,
+    for part in range(parts):
+        for k in range(depth):
+            stage[pl.ds(k, slots, stride=depth), :] = picked_rows[:, columns(part, k)]
+        rows_out[part] = stage[0 : slots * depth, :].reshape(rows_out.shape[1:]).astype(BF)
+
+        def send_rows(peer_e, peer_s, part=part):
+            pltpu.make_async_remote_copy(
+                src_ref=rows_out.at[part, peer_e],
+                dst_ref=rows_in.at[part, me],
+                send_sem=row_send.at[part],
+                recv_sem=row_recv.at[part],
+                device_id=(peer_e, peer_s),
+                device_id_type=MESH,
+            ).start()
+
+        to_all(send_rows)
+        pltpu.make_async_copy(
+            rows_out.at[part, me_e], rows_in.at[part, me], row_recv.at[part]
         ).start()
-
-    to_all(send_rows)
-    pltpu.make_async_copy(rows_out.at[me_e], rows_in.at[me], row_recv).start()
 
     gates = jax.nn.sigmoid(
         lax.dot_general(
@@ -241,64 +269,90 @@
     gate_high = gate_cols.astype(BF)
     gate_low = (gate_cols - gate_high.astype(F32)).astype(BF)
 
-    pltpu.make_async_copy(rows_in, rows_in, row_recv).wait()
-
     block = rows_x.shape[0]
     sources = block // cap
+    single = devices == sources
+
+    def rows_arrive(part):
+        pltpu.make_async_copy(rows_in.at[part], rows_in.at[part], row_recv.at[part]).wait()
+
+    def send_part(part):
+        def send_back(peer_e, peer_s):
+            pltpu.make_async_remote_copy(
+                src_ref=ret_out.at[part, peer_e * n_seq + peer_s],
+                dst_ref=ret_in.at[part, me],
+                send_sem=ret_send.at[part],
+                recv_sem=ret_recv.at[part],
+                device_id=(peer_e, peer_s),
+                device_id_type=MESH,
+            ).start()
+
+        to_all(send_back)
+        pltpu.make_async_copy(
+            ret_out.at[part, me], ret_in.at[part, me], ret_recv.at[part]
+        ).start()
 
     def apply_expert(b, carry):
         at = pl.ds(b * sources, sources)
-        stage[0 : block * pieces, :] = rows_in[at].astype(F32).reshape(block * pieces, head)
-        for k in range(pieces):
-            rows_x[:, k * head : (k + 1) * head] = stage[
-                pl.ds(k, block, stride=pieces), :
-            ].astype(BF)
-        product = jnp.dot(rows_x[...], win[...], preferred_element_type=F32)
+        product = jnp.zeros((block, win.shape[1]), F32)
+        for part in range(parts):
+            if single:
+                rows_arrive(part)
+            stage[0 : block * depth, :] = (
+                rows_in[part, at].astype(F32).reshape(block * depth, head)
+            )
+            for k in range(depth):
+                rows_x[:, columns(part, k)] = stage[pl.ds(k, block, stride=depth), :].astype(BF)
+            span = part_columns(part)
+            product += jnp.dot(rows_x[:, span], win[span, :], preferred_element_type=F32)
         units = jax.nn.gelu(product, approximate=True).astype(BF)
-        partial = jnp.dot(units, wout[...], preferred_element_type=F32)
-        for k in range(pieces):
-            stage[pl.ds(k, block, stride=pieces), :] = partial[:, k * head : (k + 1) * head]
-        ret_out[at] = stage[0 : block * pieces, :].reshape(sources, cap * pieces, head).astype(BF)
+        for part in range(parts):
+            partial = jnp.dot(units, wout[:, part_columns(part)], preferred_element_type=F32)
+            for k in range(depth):
+                stage[pl.ds(k, block, stride=depth), :] = partial[:, k * head : (k + 1) * head]
+            ret_out[part, at] = (
+                stage[0 : block * depth, :].reshape(sources, cap * depth, head).astype(BF)
+            )
+            if single:
+                send_part(part)
         return carry
 
-    if devices == sources:
+    if single:
         apply_expert(0, 0)
     else:
+        for part in range(parts):
+            rows_arrive(part)
         lax.fori_loop(0, devices // sources, apply_expert, 0)
-
-    def send_back(peer_e, peer_s):
-        pltpu.make_async_remote_copy(
-            src_ref=ret_out.at[peer_e * n_seq + peer_s],
-            dst_ref=ret_in.at[me],
-            send_sem=ret_send,
-            recv_sem=ret_recv,
-            device_id=(peer_e, peer_s),
-            device_id_type=MESH,
-        ).start()
-
-    to_all(send_back)
-    pltpu.make_async_copy(ret_out.at[me], ret_in.at[me], ret_recv).start()
-
-    for sent, _ in qkv_copies + att_copies:
-        for copy in sent:
+        for part in range(parts):
+            send_part(part)
+
+    for j in range(local_heads):
+        if not 0 < j == local_heads - 1:
+            for copy in qkv_copies[j][0]:
+                copy.wait_send()
+        for copy in att_copies[j][0]:
             copy.wait_send()
-    others = rows_in.at[pl.ds(0, devices - 1)]
-    pltpu.make_async_copy(others, others, row_send).wait()
-
-    pltpu.make_async_copy(ret_in, ret_in, ret_recv).wait()
-    for e in range(n_exp):
-        summed = jnp.sum(ret_in[e * n_seq : (e + 1) * n_seq].astype(F32), axis=0)
-        stage[e * cap * pieces : (e + 1) * cap * pieces, :] = summed
-    for k in range(pieces):
-        rows_e[:, k * head : (k + 1) * head] = stage[pl.ds(k, slots, stride=pieces), :].astype(BF)
-    expert_rows = rows_e[...]
-    mixture = jnp.dot(gate_high, expert_rows, preferred_element_type=F32) + jnp.dot(
-        gate_low, expert_rows, preferred_element_type=F32
-    )
-    out_ref[...] = (resid[...] + mod[3:4, :] * mixture).astype(BF)
-
-    others = ret_in.at[pl.ds(0, devices - 1)]
-    pltpu.make_async_copy(others, others, ret_send).wait()
+    for part in range(parts):
+        others = rows_in.at[part, pl.ds(0, devices - 1)]
+        pltpu.make_async_copy(others, others, row_send.at[part]).wait()
+
+    for part in range(parts):
+        pltpu.make_async_copy(ret_in.at[part], ret_in.at[part], ret_recv.at[part]).wait()
+        for e in range(n_exp):
+            summed = jnp.sum(ret_in[part, e * n_seq : (e + 1) * n_seq].astype(F32), axis=0)
+            stage[e * cap * depth : (e + 1) * cap * depth, :] = summed
+        for k in range(depth):
+            rows_e[:, columns(part, k)] = stage[pl.ds(k, slots, stride=depth), :].astype(BF)
+        span = part_columns(part)
+        expert_rows = rows_e[:, span]
+        mixture = jnp.dot(gate_high, expert_rows, preferred_element_type=F32) + jnp.dot(
+            gate_low, expert_rows, preferred_element_type=F32
+        )
+        out_ref[:, span] = (resid[:, span] + mod[3:4, span] * mixture).astype(BF)
+
+    for part in range(parts):
+        others = ret_in.at[part, pl.ds(0, devices - 1)]
+        pltpu.make_async_copy(others, others, ret_send.at[part]).wait()
 
 
 def per_device(
@@ -312,11 +366,12 @@
     devices = n_exp * n_seq
     slots = experts * cap
     pieces = width // head
+    parts = 1
+    depth = pieces // parts
     local_heads = heads // n_seq
     block = min(64, devices * cap)
     dma = pltpu.SemaphoreType.DMA
     anywhere = pl.BlockSpec(memory_space=pl.ANY)
-    scalars = pl.BlockSpec(memory_space=pltpu.SMEM)
     rows = toks * three * heads
     flops = (
         4 * local_heads * (toks * n_seq) ** 2 * head + 4 * devices * cap * width * units
@@ -324,9 +379,11 @@
     out = pl.pallas_call(
         functools.partial(block_kernel, n_exp, n_seq, heads, cap),
         out_shape=jax.ShapeDtypeStruct((toks, width), BF),
-        in_specs=[scalars] * 2 + [anywhere] * 6,
+        in_specs=[anywhere] * 8,
         out_specs=pl.BlockSpec(memory_space=pltpu.VMEM),
         scratch_shapes=[
+            pltpu.SMEM((cap, experts), jnp.int32),
+            pltpu.SMEM((1, experts), jnp.int32),
             pltpu.VMEM((rows, head), BF),
             pltpu.VMEM((toks, width), BF),
             pltpu.VMEM((4, width), F32),
@@ -339,24 +396,24 @@
             pltpu.VMEM((local_heads, n_seq, toks, head), BF),
             pltpu.VMEM((local_heads, n_seq, toks, head), BF),
             pltpu.VMEM((toks, width), F32),
-            pltpu.VMEM((max(block, slots) * pieces, head), F32),
-            pltpu.VMEM((experts, cap * pieces, head), BF),
-            pltpu.VMEM((devices, cap * pieces, head), BF),
+            pltpu.VMEM((max(block, slots) * depth, head), F32),
+            pltpu.VMEM((parts, experts, cap * depth, head), BF),
+            pltpu.VMEM((parts, devices, cap * depth, head), BF),
             pltpu.VMEM((block, width), BF),
-            pltpu.VMEM((devices, cap * pieces, head), BF),
-            pltpu.VMEM((devices, cap * pieces, head), BF),
+            pltpu.VMEM((parts, devices, cap * depth, head), BF),
+            pltpu.VMEM((parts, devices, cap * depth, head), BF),
             pltpu.VMEM((slots, width), BF),
-            dma((6,)),
+            dma((8,)),
             dma((local_heads, n_seq)),
             dma((local_heads, n_seq)),
             dma((local_heads,)),
             dma((local_heads, n_seq)),
             dma((local_heads, n_seq)),
             dma((local_heads,)),
-            dma,
-            dma,
-            dma,
-            dma,
+            dma((parts,)),
+            dma((parts,)),
+            dma((parts,)),
+            dma((parts,)),
         ],
         compiler_params=pltpu.CompilerParams(
             collective_id=0, has_side_effects=True, vmem_limit_bytes=56 * 1024 * 1024

time: 73.7 us -> 72.7 us (0.986)
  Pallas kernels: 71.6 us -> 70.6 us
    pallas_call x1, Pallas kernels: 71.6 us -> 70.6 us  [per_device(): pl.pallas_call(functools.partial(block_kernel, n_exp, n_seq, heads, cap),...]
where the time goes in v3:
time: 72.7 us; the launch traced here: 72.5 us
  Pallas kernels  70.6 us (97%)
  local copies, waits for them, and re-layouts  1.88 us (3%)
    pallas_call x1, Pallas kernels, per_device(): pl.pallas_call(functools.partial(block_kernel, n_exp, n_seq, heads, cap),...  70.6 us
    unnamed x1, local copies, waits for them, and re-layouts  1.88 us

profile of v3, /device:TPU:0, one launch (start us, length us, event | category | flops | bytes accessed | tf_op | source)
XLA Modules:
  0.0 72.5 jit_solution(9861947641483170425)
XLA Ops:
  0.0 70.6 %shard_map.82 = bf16[128,2048]{1,0:T(8,128)(2,1)} custom-call(s32[2,8]{1,0:T(2,128)} %bitcast.18, s32[1,8]{1,0:T(1,128)} %bitcast.19, bf16[6144,128]{1,0:T(8,128)(2,1)} %bitcast.14, bf16[128,2048]{1,0:T(8,128)(2,1)} %bitcast.15, f32[4,2048]{1,0:T(4,128)} %bitcast.16, bf16[8,2048]{1,0:T(8,128)(2,1)} %bitcast.17, bf16[2048,1024]{1,0:T(8,128)(2,1)} %bitcast.11, ...), custom_call_target="tpu_custom_call" | custom-call | flops 1073741824 | bytes 8388608 | tf_op jit(solution)/shard_map/pallas_call | solution.py:379
  70.6 1.9 %copy.10 = bf16[1,128,2048]{2,1,0:T(8,128)(2,1)} copy(bf16[1,128,2048]{2,1,0:T(8,128)(2,1)} %bitcast.13) | data formatting | bytes 1048576

commit v4 on v3

--- a/solution.py
+++ b/solution.py
@@ -159,23 +159,27 @@
     group = min(512 // toks, n_seq)
     att_copies = []
 
-    def send_back_heads(j):
-        sent = []
-        for d in range(1, n_seq):
-            peer = lax.rem(me_s + d, n_seq)
-            copy = pltpu.make_async_remote_copy(
-                src_ref=att_out.at[j, peer],
-                dst_ref=att_in.at[j, me_s],
-                send_sem=att_send.at[j, d],
-                recv_sem=att_recv.at[j, d],
-                device_id=(me_e, peer),
-                device_id_type=MESH,
-            )
-            copy.start()
-            sent.append(copy)
+    def send_heads_to(j, d):
+        peer = lax.rem(me_s + d, n_seq)
+        copy = pltpu.make_async_remote_copy(
+            src_ref=att_out.at[j, peer],
+            dst_ref=att_in.at[j, me_s],
+            send_sem=att_send.at[j, d],
+            recv_sem=att_recv.at[j, d],
+            device_id=(me_e, peer),
+            device_id_type=MESH,
+        )
+        copy.start()
+        return copy
+
+    def keep_heads(j):
         own = pltpu.make_async_copy(att_out.at[j, me_s], att_in.at[j, me_s], att_own.at[j])
         own.start()
-        att_copies.append((sent, own))
+        return own
+
+    def send_back_heads(j):
+        sent = [send_heads_to(j, d) for d in range(1, n_seq)]
+        att_copies.append((sent, keep_heads(j)))
 
     for j in range(local_heads):
         sent, own = qkv_copies[j]
@@ -188,9 +192,12 @@
         for copy in sent:
             copy.wait_recv()
 
-        def attend(b, carry, j=j):
-            at = pl.ds(b * group, group)
-            queries = qkv_in[j, 0, at].reshape(group * toks, head)
+        last = j == local_heads - 1
+        held = 1 if last else group
+
+        def attend(b, carry, j=j, held=held):
+            at = pl.ds(b * held, held)
+            queries = qkv_in[j, 0, at].reshape(held * toks, head)
             keys = qkv_in[j, 1].reshape(length, head)
             values = qkv_in[j, 2].reshape(length, head)
             scores = lax.dot_general(
@@ -200,14 +207,21 @@
             weights = jnp.exp(scores - jnp.max(scores, axis=-1, keepdims=True))
             weights = weights * (1.0 / jnp.sum(weights, axis=-1, keepdims=True))
             mixed = jnp.dot(weights.astype(BF), values, preferred_element_type=F32)
-            att_out[j, at] = mixed.astype(BF).reshape(group, toks, head)
+            att_out[j, at] = mixed.astype(BF).reshape(held, toks, head)
             return carry
 
-        if n_seq == group:
+        if last:
+            sent = []
+            for d in offsets:
+                peer = lax.rem(me_s + d, n_seq)
+                attend(peer, 0)
+                if d:
+                    sent.append(send_heads_to(j, d))
+            att_copies.append((sent, keep_heads(j)))
+        elif n_seq == group:
             attend(0, 0)
         else:
             lax.fori_loop(0, n_seq // group, attend, 0)
-    send_back_heads(local_heads - 1)
 
     for load in loads[1:6]:
         load.wait()

time: 72.7 us -> 72.8 us (level)
  no operation moved by 1% of the time
where the time goes in v4:
time: 72.8 us; the launch traced here: 72.6 us
  Pallas kernels  70.7 us (97%)
  local copies, waits for them, and re-layouts  1.88 us (3%)
    pallas_call x1, Pallas kernels, per_device(): pl.pallas_call(functools.partial(block_kernel, n_exp, n_seq, heads, cap),...  70.7 us
    unnamed x1, local copies, waits for them, and re-layouts  1.88 us

profile of v4, /device:TPU:0, one launch (start us, length us, event | category | flops | bytes accessed | tf_op | source)
XLA Modules:
  0.0 72.6 jit_solution(555192334345683009)
XLA Ops:
  0.0 70.7 %shard_map.82 = bf16[128,2048]{1,0:T(8,128)(2,1)} custom-call(s32[2,8]{1,0:T(2,128)} %bitcast.18, s32[1,8]{1,0:T(1,128)} %bitcast.19, bf16[6144,128]{1,0:T(8,128)(2,1)} %bitcast.14, bf16[128,2048]{1,0:T(8,128)(2,1)} %bitcast.15, f32[4,2048]{1,0:T(4,128)} %bitcast.16, bf16[8,2048]{1,0:T(8,128)(2,1)} %bitcast.17, bf16[2048,1024]{1,0:T(8,128)(2,1)} %bitcast.11, ...), custom_call_target="tpu_custom_call" | custom-call | flops 1073741824 | bytes 8388608 | tf_op jit(solution)/shard_map/pallas_call | solution.py:393
  70.7 1.9 %copy.10 = bf16[1,128,2048]{2,1,0:T(8,128)(2,1)} copy(bf16[1,128,2048]{2,1,0:T(8,128)(2,1)} %bitcast.13) | data formatting | bytes 1048576
